TPU v7x, 512 devices: a whole 4x4x16 slice. The times are simulated.
512 devices in a mesh: replica: 16 (over z_lo, y), section: 4 (over z_hi), tp: 8 (over x, core).
Axes of the slice: x: 4, y: 4, z: 16 (z_hi: 4, z_lo: 4; z = z_hi * 4 + z_lo), core: 2. Of those that a mesh axis runs over, the one named last changes fastest.
Arguments:
- hidden_in: bfloat16 [2048, 8192], P('replica', 'tp'), may hold values from -6 to 6
- gains: float32 [4, 8192], P('section', 'tp'), may hold values from 0.5 to 2
- weights: bfloat16 [4, 8192, 16, 512], P('section', 'tp', 'replica'), may hold values from -0.0625 to 0.0625
- lengths: int32 [16], P('replica'), may hold values from 1 to 128, 1536 in all
Outputs:
- states: bfloat16 [4, 2048, 8192], P('section', 'replica', 'tp')
Inputs may be any that keep to these rules, and one draw needn't show every extreme that they name: One replica's prompt fills all 128 slots; the lengths sum to 3 * 2048 // 4 (integer division).
All inputs are finite; a program needn't handle non-finite values. No bound on the sum of `lengths` on one device may be relied on, other than what follows from the above.
Results may differ from a plain program's by a relative error of at most 0.025.
Values may be sent and summed in bfloat16 or wider, within the bound.
A program may use at most 64 MiB of HBM per device.

v0:
```python
import jax
import jax.numpy as jnp
from jax import lax
from jax.sharding import PartitionSpec as P

MICRO = 4


EPSILON = 1e-06


def from_behind(block, axis, distance):
    devices = range(lax.axis_size(axis))
    route = [(i - distance, i) for i in devices if i - distance in devices]
    return lax.ppermute(block, axis, route)


def local(hidden_in, gains, weights, lengths):
    tok_rep = hidden_in.shape[0]
    feat_block = hidden_in.shape[1]
    groups = lax.axis_size("tp")
    page_width = weights.shape[3]
    col_width = page_width // groups
    full_width = feat_block * groups
    replicas = lax.axis_size("replica")
    w_local = weights.reshape(feat_block, page_width)
    gain_row = gains[0][None, :]
    section_id = lax.axis_index("section")
    micro_rows = tok_rep // MICRO
    all_rows = replicas * micro_rows
    rounds = MICRO + lax.axis_size("section") - 1
    handed = jnp.zeros((micro_rows, feat_block), jnp.bfloat16)
    collected = jnp.zeros((MICRO, micro_rows, feat_block), jnp.bfloat16)
    for round_now in range(rounds):
        lower = min(round_now, MICRO - 1) * micro_rows
        incoming = hidden_in[lower : lower + micro_rows]
        current = jnp.where(section_id == 0, incoming, handed)
        widened = current.astype(jnp.float32)
        squares_sum = lax.psum(jnp.sum(widened * widened, axis=1), "tp")
        inverse = lax.rsqrt(squares_sum / full_width + EPSILON)
        scaled = (widened * gain_row).astype(jnp.bfloat16)
        partial_value = jnp.dot(
            lax.all_gather(scaled, "replica", axis=0, tiled=True),
            w_local,
            preferred_element_type=jnp.float32,
        )
        summed = lax.psum_scatter(
            partial_value.reshape(all_rows, groups, col_width).astype(jnp.bfloat16),
            "tp",
            scatter_dimension=1,
            tiled=True,
        ).astype(jnp.float32)
        own_rows = lax.all_to_all(
            summed.reshape(all_rows, col_width).astype(jnp.bfloat16),
            "replica",
            split_axis=0,
            concat_axis=1,
            tiled=True,
        ).astype(jnp.float32)
        updated = (widened + inverse[:, None] * own_rows).astype(jnp.bfloat16)
        slot_now = round_now - section_id
        in_range = (slot_now >= 0) & (slot_now < MICRO)
        slot_index = jnp.clip(slot_now, 0, MICRO - 1)
        placed = lax.dynamic_update_index_in_dim(collected, updated, slot_index, 0)
        collected = jnp.where(in_range, placed, collected)
        if round_now + 1 < rounds:
            handed = from_behind(updated, "section", 1)
    flat_states = collected.reshape(tok_rep, feat_block)
    positions = jnp.arange(tok_rep, dtype=jnp.int32)
    masked = jnp.where((positions < lengths[0])[:, None], flat_states, jnp.zeros_like(flat_states))
    return masked[None]


def solution(mesh):
    return jax.shard_map(
        local,
        mesh=mesh,
        in_specs=(
            P("replica", "tp"),
            P("section", "tp"),
            P("section", "tp", "replica", None),
            P("replica"),
        ),
        out_specs=P("section", "replica", "tp"),
        check_vma=False,
    )
```

profile of v0, /device:TPU:481, one launch (start us, length us, event | category | flops | bytes accessed | tf_op | source)
XLA Modules:
  0.0 1124.5 jit_solution(7788064302229757777)
XLA Ops:
  10.4 69.0 %all-gather.8.cloned.1.call-done = bf16[512,1024]{1,0:T(8,128)(2,1)} async-done(((bf16[32,1024]{1,0:T(8,128)(2,1)}), bf16[512,1024]{1,0:T(8,128)(2,1)}) %all-gather.8.cloned.1.call-update) | async-done | bytes 1048592 | tf_op jit(solution)/shard_map/all_gather | solution.py:43
  82.3 49.7 %reduce-scatter.8.cloned.1.call-done = bf16[512,1,64]{0,2,1:T(8,128)(2,1)} async-done(((bf16[512,8,64]{0,2,1:T(8,128)(2,1)}), bf16[512,1,64]{0,2,1:T(8,128)(2,1)}) %reduce-scatter.8.cloned.1.call-update) | async-done | bytes 65552 | tf_op jit(solution)/shard_map/reduce_scatter | solution.py:47
  133.7 7.0 all-to-all-start
  140.7 15.6 %psum.49 = f32[32]{0:T(128)S(1)} all-reduce(f32[32]{0:T(128)S(1)} %get-tuple-element.29), channel_id=1, replica_groups=mesh['replica'=16,'section'=4,'tp'=8] {'tp'}, use_global_device_ids=true, to_apply=%region_1.2 | all-reduce | flops 32 | bytes 256 | tf_op jit(solution)/shard_map/psum | solution.py:39
  159.0 12.3 %collective-permute-done = bf16[32,1024]{1,0:T(8,128)(2,1)S(1)} collective-permute-done((bf16[32,1024]{1,0:T(8,128)(2,1)S(1)}, bf16[32,1024]{1,0:T(8,128)(2,1)S(1)}, u32[]{:S(2)}, u32[]{:S(2)}) %collective-permute-start) | collective-permute-done | bytes 65568 | tf_op jit(solution)/shard_map/ppermute | solution.py:15
  172.1 68.1 %all-gather.10.cloned.1.call-done = bf16[512,1024]{1,0:T(8,128)(2,1)} async-done(((bf16[32,1024]{1,0:T(8,128)(2,1)}), bf16[512,1024]{1,0:T(8,128)(2,1)}) %all-gather.10.cloned.1.call-update) | async-done | bytes 1048592 | tf_op jit(solution)/shard_map/all_gather | solution.py:43
  243.0 49.6 %reduce-scatter.10.cloned.1.call-done = bf16[512,1,64]{0,2,1:T(8,128)(2,1)} async-done(((bf16[512,8,64]{0,2,1:T(8,128)(2,1)}), bf16[512,1,64]{0,2,1:T(8,128)(2,1)}) %reduce-scatter.10.cloned.1.call-update) | async-done | bytes 65552 | tf_op jit(solution)/shard_map/reduce_scatter | solution.py:47
  294.4 7.0 all-to-all-start.1
  301.4 15.6 %psum.50 = f32[32]{0:T(128)S(1)} all-reduce(f32[32]{0:T(128)S(1)} %get-tuple-element.25), channel_id=1, replica_groups=mesh['replica'=16,'section'=4,'tp'=8] {'tp'}, use_global_device_ids=true, to_apply=%region_4.5 | all-reduce | flops 32 | bytes 256 | tf_op jit(solution)/shard_map/psum | solution.py:39
  318.9 12.3 %collective-permute-done.1 = bf16[32,1024]{1,0:T(8,128)(2,1)S(1)} collective-permute-done((bf16[32,1024]{1,0:T(8,128)(2,1)S(1)}, bf16[32,1024]{1,0:T(8,128)(2,1)S(1)}, u32[]{:S(2)}, u32[]{:S(2)}) %collective-permute-start.1) | collective-permute-done | bytes 65568 | tf_op jit(solution)/shard_map/ppermute | solution.py:15
  332.0 68.1 %all-gather.12.cloned.1.call-done = bf16[512,1024]{1,0:T(8,128)(2,1)} async-done(((bf16[32,1024]{1,0:T(8,128)(2,1)}), bf16[512,1024]{1,0:T(8,128)(2,1)}) %all-gather.12.cloned.1.call-update) | async-done | bytes 1048592 | tf_op jit(solution)/shard_map/all_gather | solution.py:43
  402.9 49.7 %reduce-scatter.12.cloned.1.call-done = bf16[512,1,64]{0,2,1:T(8,128)(2,1)} async-done(((bf16[512,8,64]{0,2,1:T(8,128)(2,1)}), bf16[512,1,64]{0,2,1:T(8,128)(2,1)}) %reduce-scatter.12.cloned.1.call-update) | async-done | bytes 65552 | tf_op jit(solution)/shard_map/reduce_scatter | solution.py:47
  461.3 15.6 %psum.51 = f32[32]{0:T(128)S(1)} all-reduce(f32[32]{0:T(128)S(1)} %get-tuple-element.21), channel_id=1, replica_groups=mesh['replica'=16,'section'=4,'tp'=8] {'tp'}, use_global_device_ids=true, to_apply=%region_7.8 | all-reduce | flops 32 | bytes 256 | tf_op jit(solution)/shard_map/psum | solution.py:39
  478.8 12.3 %collective-permute-done.2 = bf16[32,1024]{1,0:T(8,128)(2,1)S(1)} collective-permute-done((bf16[32,1024]{1,0:T(8,128)(2,1)S(1)}, bf16[32,1024]{1,0:T(8,128)(2,1)S(1)}, u32[]{:S(2)}, u32[]{:S(2)}) %collective-permute-start.2) | collective-permute-done | bytes 65568 | tf_op jit(solution)/shard_map/ppermute | solution.py:15
  491.9 68.1 %all-gather.14.cloned.1.call-done = bf16[512,1024]{1,0:T(8,128)(2,1)} async-done(((bf16[32,1024]{1,0:T(8,128)(2,1)}), bf16[512,1024]{1,0:T(8,128)(2,1)}) %all-gather.14.cloned.1.call-update) | async-done | bytes 1048592 | tf_op jit(solution)/shard_map/all_gather | solution.py:43
  562.9 49.7 %reduce-scatter.14.cloned.1.call-done = bf16[512,1,64]{0,2,1:T(8,128)(2,1)} async-done(((bf16[512,8,64]{0,2,1:T(8,128)(2,1)}), bf16[512,1,64]{0,2,1:T(8,128)(2,1)}) %reduce-scatter.14.cloned.1.call-update) | async-done | bytes 65552 | tf_op jit(solution)/shard_map/reduce_scatter | solution.py:47
  614.3 6.9 all-to-all-start.3
  621.3 15.6 %psum.52 = f32[32]{0:T(128)S(1)} all-reduce(f32[32]{0:T(128)S(1)} %get-tuple-element.17), channel_id=1, replica_groups=mesh['replica'=16,'section'=4,'tp'=8] {'tp'}, use_global_device_ids=true, to_apply=%region_10.11 | all-reduce | flops 32 | bytes 256 | tf_op jit(solution)/shard_map/psum | solution.py:39
  638.8 12.3 %collective-permute-done.3 = bf16[32,1024]{1,0:T(8,128)(2,1)S(1)} collective-permute-done((bf16[32,1024]{1,0:T(8,128)(2,1)S(1)}, bf16[32,1024]{1,0:T(8,128)(2,1)S(1)}, u32[]{:S(2)}, u32[]{:S(2)}) %collective-permute-start.3) | collective-permute-done | bytes 65568 | tf_op jit(solution)/shard_map/ppermute | solution.py:15
  651.9 68.1 %all-gather.16.cloned.1.call-done = bf16[512,1024]{1,0:T(8,128)(2,1)} async-done(((bf16[32,1024]{1,0:T(8,128)(2,1)}), bf16[512,1024]{1,0:T(8,128)(2,1)}) %all-gather.16.cloned.1.call-update) | async-done | bytes 1048592 | tf_op jit(solution)/shard_map/all_gather | solution.py:43
  722.9 49.6 %reduce-scatter.16.cloned.1.call-done = bf16[512,1,64]{0,2,1:T(8,128)(2,1)} async-done(((bf16[512,8,64]{0,2,1:T(8,128)(2,1)}), bf16[512,1,64]{0,2,1:T(8,128)(2,1)}) %reduce-scatter.16.cloned.1.call-update) | async-done | bytes 65552 | tf_op jit(solution)/shard_map/reduce_scatter | solution.py:47
  774.2 7.0 all-to-all-start.4
  781.3 15.6 %psum.53 = f32[32]{0:T(128)S(1)} all-reduce(f32[32]{0:T(128)S(1)} %get-tuple-element.13), channel_id=1, replica_groups=mesh['replica'=16,'section'=4,'tp'=8] {'tp'}, use_global_device_ids=true, to_apply=%region_13.14 | all-reduce | flops 32 | bytes 256 | tf_op jit(solution)/shard_map/psum | solution.py:39
  798.7 12.3 %collective-permute-done.4 = bf16[32,1024]{1,0:T(8,128)(2,1)S(1)} collective-permute-done((bf16[32,1024]{1,0:T(8,128)(2,1)S(1)}, bf16[32,1024]{1,0:T(8,128)(2,1)S(1)}, u32[]{:S(2)}, u32[]{:S(2)}) %collective-permute-start.4) | collective-permute-done | bytes 65568 | tf_op jit(solution)/shard_map/ppermute | solution.py:15
  811.8 68.0 %all-gather.18.cloned.1.call-done = bf16[512,1024]{1,0:T(8,128)(2,1)} async-done(((bf16[32,1024]{1,0:T(8,128)(2,1)}), bf16[512,1024]{1,0:T(8,128)(2,1)}) %all-gather.18.cloned.1.call-update) | async-done | bytes 1048592 | tf_op jit(solution)/shard_map/all_gather | solution.py:43
  882.7 49.6 %reduce-scatter.18.cloned.1.call-done = bf16[512,1,64]{0,2,1:T(8,128)(2,1)} async-done(((bf16[512,8,64]{0,2,1:T(8,128)(2,1)}), bf16[512,1,64]{0,2,1:T(8,128)(2,1)}) %reduce-scatter.18.cloned.1.call-update) | async-done | bytes 65552 | tf_op jit(solution)/shard_map/reduce_scatter | solution.py:47
  934.0 7.0 all-to-all-start.5
  941.1 15.6 %psum.54 = f32[32]{0:T(128)S(1)} all-reduce(f32[32]{0:T(128)S(1)} %get-tuple-element.9), channel_id=1, replica_groups=mesh['replica'=16,'section'=4,'tp'=8] {'tp'}, use_global_device_ids=true, to_apply=%region_16.17 | all-reduce | flops 32 | bytes 256 | tf_op jit(solution)/shard_map/psum | solution.py:39
  958.6 12.3 %collective-permute-done.5 = bf16[32,1024]{1,0:T(8,128)(2,1)S(1)} collective-permute-done((bf16[32,1024]{1,0:T(8,128)(2,1)S(1)}, bf16[32,1024]{1,0:T(8,128)(2,1)S(1)}, u32[]{:S(2)}, u32[]{:S(2)}) %collective-permute-start.5) | collective-permute-done | bytes 65568 | tf_op jit(solution)/shard_map/ppermute | solution.py:15
  971.7 68.1 %all-gather.20.cloned.1.call-done = bf16[512,1024]{1,0:T(8,128)(2,1)} async-done(((bf16[32,1024]{1,0:T(8,128)(2,1)}), bf16[512,1024]{1,0:T(8,128)(2,1)}) %all-gather.20.cloned.1.call-update) | async-done | bytes 1048592 | tf_op jit(solution)/shard_map/all_gather | solution.py:43
  1043.3 49.0 %reduce-scatter.20.cloned.1.call-done = bf16[512,1,64]{0,2,1:T(8,128)(2,1)} async-done(((bf16[512,8,64]{0,2,1:T(8,128)(2,1)}), bf16[512,1,64]{0,2,1:T(8,128)(2,1)}) %reduce-scatter.20.cloned.1.call-update) | async-done | bytes 65552 | tf_op jit(solution)/shard_map/reduce_scatter | solution.py:47
  1101.0 15.6 %psum.55 = f32[32]{0:T(128)S(1)} all-reduce(f32[32]{0:T(128)S(1)} %get-tuple-element.5), channel_id=1, replica_groups=mesh['replica'=16,'section'=4,'tp'=8] {'tp'}, use_global_device_ids=true, to_apply=%region_19.20 | all-reduce | flops 32 | bytes 256 | tf_op jit(solution)/shard_map/psum | solution.py:39
  (127 shorter events, 68.0 us)
Async XLA Ops:
  6.5 72.9 %all-gather.8.cloned.1.call-start = ((), (), s32[]{:S(2)}) async-start(), calls=%async_computation.14 | async-start | bytes 1114112 | tf_op jit(solution)/shard_map/all_gather | solution.py:43
  6.5 0.7 copy-start.1
  8.9 123.1 %reduce-scatter.8.cloned.1.call-start = ((), (), s32[]{:S(2)}) async-start(), calls=%async_computation.15 | async-start | bytes 589824 | tf_op jit(solution)/shard_map/reduce_scatter | solution.py:47
  133.7 22.6 %all-to-all-start = ((bf16[16,2,1024]{2,1,0:T(2,128)(2,1)}), bf16[16,2,1024]{2,1,0:T(2,128)(2,1)S(1)}, u32[]{:S(2)}, u32[]{:S(2)}) async-start(bf16[16,2,1024]{2,1,0:T(2,128)(2,1)} %reshape.133), calls=%async_computation.1 | async-start | bytes 131072 | tf_op jit(solution)/shard_map/all_to_all | solution.py:53
  140.7 99.5 %all-gather.10.cloned.1.call-start = ((), (), s32[]{:S(2)}) async-start(), calls=%async_computation.16 | async-start | bytes 1114112 | tf_op jit(solution)/shard_map/all_gather | solution.py:43
  156.7 1.0 copy-start
  157.7 13.6 %collective-permute-start = (bf16[32,1024]{1,0:T(8,128)(2,1)S(1)}, bf16[32,1024]{1,0:T(8,128)(2,1)S(1)}, u32[]{:S(2)}, u32[]{:S(2)}) collective-permute-start(bf16[32,1024]{1,0:T(8,128)(2,1)S(1)} %get-tuple-element.28), channel_id=1, source_target_pairs={{0,8},{8,16},{16,24},{1,9},{9,17},{17,25},{2,10},{10,18},{18,26},{... | collective-permute-start | bytes 196616 | tf_op jit(solution)/shard_map/ppermute | solution.py:15
  172.1 120.5 %reduce-scatter.10.cloned.1.call-start = ((), (), s32[]{:S(2)}) async-start(), calls=%async_computation.17 | async-start | bytes 589824 | tf_op jit(solution)/shard_map/reduce_scatter | solution.py:47
  294.4 22.7 %all-to-all-start.1 = ((bf16[16,2,1024]{2,1,0:T(2,128)(2,1)}), bf16[16,2,1024]{2,1,0:T(2,128)(2,1)S(1)}, u32[]{:S(2)}, u32[]{:S(2)}) async-start(bf16[16,2,1024]{2,1,0:T(2,128)(2,1)} %reshape.135), calls=%async_computation.3 | async-start | bytes 131072 | tf_op jit(solution)/shard_map/all_to_all | solution.py:53
  301.3 98.8 %all-gather.12.cloned.1.call-start = ((), (), s32[]{:S(2)}) async-start(), calls=%async_computation.18 | async-start | bytes 1114112 | tf_op jit(solution)/shard_map/all_gather | solution.py:43
  317.6 13.6 %collective-permute-start.1 = (bf16[32,1024]{1,0:T(8,128)(2,1)S(1)}, bf16[32,1024]{1,0:T(8,128)(2,1)S(1)}, u32[]{:S(2)}, u32[]{:S(2)}) collective-permute-start(bf16[32,1024]{1,0:T(8,128)(2,1)S(1)} %get-tuple-element.24), channel_id=1, source_target_pairs={{0,8},{8,16},{16,24},{1,9},{9,17},{17,25},{2,10},{10,18},{18,26},{... | collective-permute-start | bytes 196616 | tf_op jit(solution)/shard_map/ppermute | solution.py:15
  332.0 120.6 %reduce-scatter.12.cloned.1.call-start = ((), (), s32[]{:S(2)}) async-start(), calls=%async_computation.19 | async-start | bytes 589824 | tf_op jit(solution)/shard_map/reduce_scatter | solution.py:47
  454.4 22.6 %all-to-all-start.2 = ((bf16[16,2,1024]{2,1,0:T(2,128)(2,1)}), bf16[16,2,1024]{2,1,0:T(2,128)(2,1)S(1)}, u32[]{:S(2)}, u32[]{:S(2)}) async-start(bf16[16,2,1024]{2,1,0:T(2,128)(2,1)} %reshape.137), calls=%async_computation.5 | async-start | bytes 131072 | tf_op jit(solution)/shard_map/all_to_all | solution.py:53
  461.3 98.8 %all-gather.14.cloned.1.call-start = ((), (), s32[]{:S(2)}) async-start(), calls=%async_computation.20 | async-start | bytes 1114112 | tf_op jit(solution)/shard_map/all_gather | solution.py:43
  477.5 13.6 %collective-permute-start.2 = (bf16[32,1024]{1,0:T(8,128)(2,1)S(1)}, bf16[32,1024]{1,0:T(8,128)(2,1)S(1)}, u32[]{:S(2)}, u32[]{:S(2)}) collective-permute-start(bf16[32,1024]{1,0:T(8,128)(2,1)S(1)} %get-tuple-element.20), channel_id=1, source_target_pairs={{0,8},{8,16},{16,24},{1,9},{9,17},{17,25},{2,10},{10,18},{18,26},{... | collective-permute-start | bytes 196616 | tf_op jit(solution)/shard_map/ppermute | solution.py:15
  491.9 120.7 %reduce-scatter.14.cloned.1.call-start = ((), (), s32[]{:S(2)}) async-start(), calls=%async_computation.21 | async-start | bytes 589824 | tf_op jit(solution)/shard_map/reduce_scatter | solution.py:47
  614.3 22.6 %all-to-all-start.3 = ((bf16[16,2,1024]{2,1,0:T(2,128)(2,1)}), bf16[16,2,1024]{2,1,0:T(2,128)(2,1)S(1)}, u32[]{:S(2)}, u32[]{:S(2)}) async-start(bf16[16,2,1024]{2,1,0:T(2,128)(2,1)} %reshape.139), calls=%async_computation.7 | async-start | bytes 131072 | tf_op jit(solution)/shard_map/all_to_all | solution.py:53
  621.3 98.8 %all-gather.16.cloned.1.call-start = ((), (), s32[]{:S(2)}) async-start(), calls=%async_computation.22 | async-start | bytes 1114112 | tf_op jit(solution)/shard_map/all_gather | solution.py:43
  637.5 13.6 %collective-permute-start.3 = (bf16[32,1024]{1,0:T(8,128)(2,1)S(1)}, bf16[32,1024]{1,0:T(8,128)(2,1)S(1)}, u32[]{:S(2)}, u32[]{:S(2)}) collective-permute-start(bf16[32,1024]{1,0:T(8,128)(2,1)S(1)} %get-tuple-element.16), channel_id=1, source_target_pairs={{0,8},{8,16},{16,24},{1,9},{9,17},{17,25},{2,10},{10,18},{18,26},{... | collective-permute-start | bytes 196616 | tf_op jit(solution)/shard_map/ppermute | solution.py:15
  651.9 120.6 %reduce-scatter.16.cloned.1.call-start = ((), (), s32[]{:S(2)}) async-start(), calls=%async_computation.23 | async-start | bytes 589824 | tf_op jit(solution)/shard_map/reduce_scatter | solution.py:47
  774.2 22.6 %all-to-all-start.4 = ((bf16[16,2,1024]{2,1,0:T(2,128)(2,1)}), bf16[16,2,1024]{2,1,0:T(2,128)(2,1)S(1)}, u32[]{:S(2)}, u32[]{:S(2)}) async-start(bf16[16,2,1024]{2,1,0:T(2,128)(2,1)} %reshape.141), calls=%async_computation.9 | async-start | bytes 131072 | tf_op jit(solution)/shard_map/all_to_all | solution.py:53
  781.2 98.7 %all-gather.18.cloned.1.call-start = ((), (), s32[]{:S(2)}) async-start(), calls=%async_computation.24 | async-start | bytes 1114112 | tf_op jit(solution)/shard_map/all_gather | solution.py:43
  797.4 13.6 %collective-permute-start.4 = (bf16[32,1024]{1,0:T(8,128)(2,1)S(1)}, bf16[32,1024]{1,0:T(8,128)(2,1)S(1)}, u32[]{:S(2)}, u32[]{:S(2)}) collective-permute-start(bf16[32,1024]{1,0:T(8,128)(2,1)S(1)} %get-tuple-element.12), channel_id=1, source_target_pairs={{0,8},{8,16},{16,24},{1,9},{9,17},{17,25},{2,10},{10,18},{18,26},{... | collective-permute-start | bytes 196616 | tf_op jit(solution)/shard_map/ppermute | solution.py:15
  811.8 120.5 %reduce-scatter.18.cloned.1.call-start = ((), (), s32[]{:S(2)}) async-start(), calls=%async_computation.25 | async-start | bytes 589824 | tf_op jit(solution)/shard_map/reduce_scatter | solution.py:47
  934.0 22.7 %all-to-all-start.5 = ((bf16[16,2,1024]{2,1,0:T(2,128)(2,1)}), bf16[16,2,1024]{2,1,0:T(2,128)(2,1)S(1)}, u32[]{:S(2)}, u32[]{:S(2)}) async-start(bf16[16,2,1024]{2,1,0:T(2,128)(2,1)} %reshape.143), calls=%async_computation.11 | async-start | bytes 131072 | tf_op jit(solution)/shard_map/all_to_all | solution.py:53
  941.0 98.8 %all-gather.20.cloned.1.call-start = ((), (), s32[]{:S(2)}) async-start(), calls=%async_computation.26 | async-start | bytes 1114112 | tf_op jit(solution)/shard_map/all_gather | solution.py:43
  957.3 13.6 %collective-permute-start.5 = (bf16[32,1024]{1,0:T(8,128)(2,1)S(1)}, bf16[32,1024]{1,0:T(8,128)(2,1)S(1)}, u32[]{:S(2)}, u32[]{:S(2)}) collective-permute-start(bf16[32,1024]{1,0:T(8,128)(2,1)S(1)} %get-tuple-element.8), channel_id=1, source_target_pairs={{0,8},{8,16},{16,24},{1,9},{9,17},{17,25},{2,10},{10,18},{18,26},{... | collective-permute-start | bytes 196616 | tf_op jit(solution)/shard_map/ppermute | solution.py:15
  971.6 120.6 %reduce-scatter.20.cloned.1.call-start = ((), (), s32[]{:S(2)}) async-start(), calls=%async_computation.27 | async-start | bytes 589824 | tf_op jit(solution)/shard_map/reduce_scatter | solution.py:47
  1094.0 22.6 %all-to-all-start.6 = ((bf16[16,2,1024]{2,1,0:T(2,128)(2,1)}), bf16[16,2,1024]{2,1,0:T(2,128)(2,1)S(1)}, u32[]{:S(2)}, u32[]{:S(2)}) async-start(bf16[16,2,1024]{2,1,0:T(2,128)(2,1)} %reshape.145), calls=%async_computation.13 | async-start | bytes 131072 | tf_op jit(solution)/shard_map/all_to_all | solution.py:53
Sparse Core Ops, SparseCore 0:
  9.4 69.9 all-gather.7
  82.4 49.5 reduce-scatter.7
  172.2 67.9 all-gather.9
  243.1 49.4 reduce-scatter.9
  332.1 67.9 all-gather.11
  403.1 49.5 reduce-scatter.11
  492.0 67.9 all-gather.13
  563.1 49.4 reduce-scatter.13
  652.0 67.9 all-gather.15
  723.0 49.4 reduce-scatter.15
  811.9 67.9 all-gather.17
  882.8 49.4 reduce-scatter.17
  971.8 67.9 all-gather.19
  1042.7 49.5 reduce-scatter.19
where the time goes:
time: 1130 us; the launch traced here: 1120 us
  waiting for transfers between devices  898 us (79%)
  blocking collectives  109 us (10%)
  starting transfers between devices  57 us (5%)
  matrix products  19.6 us (2%)
  local copies, waits for them, and re-layouts  18.1 us (2%)
  between operations  14.3 us (1%)
    all_gather x7, waiting for transfers between devices, local(): lax.all_gather(scaled, 'replica', axis=0, tiled=True)  477 us
    reduce_scatter x7, waiting for transfers between devices, local(): lax.psum_scatter(partial_value.reshape(all_rows, groups, col_width).astyp...  347 us
    psum x7, blocking collectives, local(): squares_sum = lax.psum(jnp.sum(widened * widened, axis=1), 'tp')  109 us
    ppermute x6, waiting for transfers between devices, from_behind(): return lax.ppermute(block, axis, route)  73.6 us
    all_to_all x7, starting transfers between devices, local(): lax.all_to_all(summed.reshape(all_rows, col_width).astype(jnp.bfloat16),...  48.7 us
  transfers between devices with their start and end apart: 27, of which 20 were waited for; matrix products, arithmetic and copies ran while one was open for 0% of the time, Pallas kernels for 0%

commit v1 on v0

v1 whole, which is shorter than its diff:
```python
import functools

import jax
import jax.numpy as jnp
from jax import lax
from jax.experimental import pallas as pl
from jax.experimental.pallas import tpu as pltpu
from jax.sharding import PartitionSpec as P

EPSILON = 1e-06
MESH = pl.DeviceIdType.MESH
NEAR_Y = 4
CORES = 2
ROWS = 16
LANES = 128

STAGES = dict(scale=0.0, along_y=3.0, onward=6.5, product=9.0, pair=10.5, along_x=14.0, update=17.0)
INTERVAL = 5.0


def order_of(slabs):
    events = [
        (slab * INTERVAL + offset, slab, name)
        for slab in range(slabs)
        for name, offset in STAGES.items()
    ]
    return [(name, slab) for _, slab, name in sorted(events, key=lambda e: (e[0], e[1]))]


def kernel(
    sizes, hid_ref, gain_ref, w_ref, out_ref,
    held, gathered, squares, own, core_out, core_in, x_out, x_in, page_out, page_in, inverse,
    hop_s, hop_r, z_s, z_r, y_s, y_r, f_s, f_r, c_s, c_r, x_s, x_r, p_s, p_r,
):
    replicas, sections, groups, slabs = sizes
    near_y, near_z, near_x = NEAR_Y, replicas // NEAR_Y, groups // CORES
    half_y, half_z = near_y // 2, near_z // 2
    share = half_y * near_z
    width = hid_ref.shape[1]
    page = w_ref.shape[1]
    half_rows = share * ROWS

    replica, section, tp = lax.axis_index("replica"), lax.axis_index("section"), lax.axis_index("tp")
    z, y = replica // near_y, replica % near_y
    x, core = tp // CORES, tp % CORES
    other = 1 - core
    up_y, down_y = (y + 1) % near_y, (y + near_y - 1) % near_y

    def place(z_to=z, y_to=y, x_to=x, core_to=core, section_to=section):
        return (z_to * near_y + y_to, section_to, x_to * CORES + core_to)

    def send(src, dst, send_sem, recv_sem, device):
        pltpu.make_async_remote_copy(
            src_ref=src, dst_ref=dst, send_sem=send_sem, recv_sem=recv_sem, device_id=device, device_id_type=MESH
        ).start()

    def wait(ref, sem):
        pltpu.make_async_copy(ref, ref, sem).wait()

    lane = lax.broadcasted_iota(jnp.int32, (ROWS, LANES), 1)
    low = lane < LANES // 2

    def two_parts(value):
        high = value.astype(jnp.bfloat16).astype(jnp.float32)
        return jnp.where(low, high, value - high)

    def one_value(parts):
        return parts + pltpu.roll(parts, LANES // 2, 1)

    barrier = pltpu.get_barrier_semaphore()

    def greet(device):
        pl.semaphore_signal(barrier, inc=1, device_id=device, device_id_type=MESH)

    greeted = 0
    for dz in range(near_z):
        for dy in range(near_y):
            for dc in range(CORES):
                if dz or dy or dc:
                    greet(place((z + dz) % near_z, (y + dy) % near_y, core_to=(core + dc) % CORES))
                    greeted += 1
    for dx in range(1, near_x):
        greet(place(x_to=(x + dx) % near_x))
        greeted += 1

    @pl.when(section > 0)
    def _():
        greet(place(section_to=section - 1))

    @pl.when(section == 0)
    def _():
        held[...] = hid_ref[...].reshape(held.shape)

    pl.semaphore_wait(barrier, greeted + jnp.where(section < sections - 1, 1, 0))

    def scale(m):
        @pl.when(section > 0)
        def _():
            wait(held.at[m], hop_r.at[m])

        rows = held[m].astype(jnp.float32)
        total = jnp.sum(rows * rows, axis=1, keepdims=True)
        squares[m] = two_parts(jnp.broadcast_to(total, (ROWS, LANES)))
        gathered[m, y, z] = (rows * gain_ref[...]).astype(jnp.bfloat16)
        for dz in range(1, near_z):
            block = gathered.at[m, y, z]
            send(block, block, z_s.at[m], z_r.at[m], place(z_to=(z + dz) % near_z))

    def along_y(m):
        wait(gathered.at[m, y, pl.ds(0, near_z - 1)], z_r.at[m])
        block = gathered.at[m, y]
        send(block, block, y_s.at[m, 0], y_r.at[m, 0], place(y_to=up_y))
        send(block, block, y_s.at[m, 1], y_r.at[m, 1], place(y_to=down_y))

    def onward(m):
        wait(gathered.at[m, down_y], y_r.at[m, 0])
        block = gathered.at[m, down_y, pl.ds(0, half_z)]
        send(block, block, f_s.at[m, 0], f_r.at[m, 0], place(y_to=up_y))
        wait(gathered.at[m, up_y], y_r.at[m, 1])
        block = gathered.at[m, up_y, pl.ds(half_z, half_z)]
        send(block, block, f_s.at[m, 1], f_r.at[m, 1], place(y_to=down_y))

    def product(m):
        opposite = (y + 2) % near_y
        wait(gathered.at[m, opposite, pl.ds(0, half_z)], f_r.at[m, 0])
        wait(gathered.at[m, opposite, pl.ds(half_z, half_z)], f_r.at[m, 1])

        def times(core_of):
            rows = gathered[m, pl.ds(core_of * half_y, half_y)].reshape(half_rows, width)
            return jnp.dot(rows, w_ref[...], preferred_element_type=jnp.float32)

        core_out[m, pl.ds(0, half_rows)] = times(other).astype(jnp.bfloat16)
        core_out[m, pl.ds(half_rows, ROWS)] = jnp.concatenate(
            [squares[m].astype(jnp.bfloat16)] * (page // LANES), axis=1
        )
        send(core_out.at[m], core_in.at[m], c_s.at[m], c_r.at[m], place(core_to=other))
        own[m] = times(core)

    def pair(m):
        wait(core_in.at[m], c_r.at[m])
        total = (own[m] + core_in[m, pl.ds(0, half_rows)].astype(jnp.float32)).astype(jnp.bfloat16)
        parts = squares[m] + core_in[m, pl.ds(half_rows, ROWS), pl.ds(0, LANES)].astype(jnp.float32)
        parts = two_parts(one_value(parts)).astype(jnp.bfloat16)
        for j in range(near_x):
            x_out[m, j, pl.ds(0, half_rows)] = total[:, j * LANES : (j + 1) * LANES]
            x_out[m, j, pl.ds(half_rows, ROWS)] = parts
        for dx in range(1, near_x):
            to = (x + dx) % near_x
            send(x_out.at[m, to], x_in.at[m, dx - 1], x_s.at[m], x_r.at[m], place(x_to=to))

    def along_x(m):
        wait(x_in.at[m], x_r.at[m])
        total = x_out[m, x].astype(jnp.float32)
        for dx in range(1, near_x):
            total += x_in[m, dx - 1].astype(jnp.float32)
        page_out[m] = total[:half_rows].astype(jnp.bfloat16).reshape(share, ROWS, LANES)
        mean = one_value(total[half_rows:]) / (width * groups)
        inverse[m] = lax.rsqrt(mean + EPSILON)
        for j in range(share):
            z_to, y_to = j % near_z, core * half_y + j // near_z
            src, dst = page_out.at[m, j], page_in.at[m, replica]
            here = (z_to == z) & (y_to == y)

            @pl.when(here)
            def _(src=src, dst=dst):
                pltpu.make_async_copy(src, dst, p_r.at[m]).start()

            @pl.when(jnp.logical_not(here))
            def _(src=src, dst=dst, z_to=z_to, y_to=y_to):
                send(src, dst, p_s.at[m], p_r.at[m], place(z_to, y_to))

            send(src, dst, p_s.at[m], p_r.at[m], place(z_to, y_to, core_to=other))

    def update(m):
        wait(page_in.at[m], p_r.at[m])
        first = core == 0
        for k in range(replicas // 2):
            even = page_in[m, 2 * k].astype(jnp.float32)
            odd = page_in[m, 2 * k + 1].astype(jnp.float32)
            turned = pltpu.roll(jnp.where(first, odd, even), LANES // 2, 1)
            block = jnp.where(low, jnp.where(first, even, turned), jnp.where(first, turned, odd))
            columns = pl.ds(k * LANES, LANES)
            new = held[m, :, columns].astype(jnp.float32) + inverse[m] * block
            out_ref[pl.ds(m * ROWS, ROWS), columns] = new.astype(jnp.bfloat16)

        @pl.when(section < sections - 1)
        def _():
            send(
                out_ref.at[pl.ds(m * ROWS, ROWS)], held.at[m], hop_s.at[m], hop_r.at[m],
                place(section_to=section + 1),
            )

    stages = dict(scale=scale, along_y=along_y, onward=onward, product=product, pair=pair, along_x=along_x, update=update)
    for name, m in order_of(slabs):
        with jax.named_scope(name):
            stages[name](m)

    among = y // half_y == core
    for m in range(slabs):
        wait(gathered.at[m, 0, pl.ds(0, near_z - 1)], z_s.at[m])
        for way in range(2):
            wait(gathered.at[m, 0], y_s.at[m, way])
            wait(gathered.at[m, 0, pl.ds(0, half_z)], f_s.at[m, way])
        wait(core_out.at[m], c_s.at[m])
        wait(x_in.at[m], x_s.at[m])

        @pl.when(among)
        def _(m=m):
            wait(page_in.at[m, pl.ds(0, CORES * share - 1)], p_s.at[m])

        @pl.when(jnp.logical_not(among))
        def _(m=m):
            wait(page_in.at[m], p_s.at[m])

        @pl.when(section < sections - 1)
        def _(m=m):
            wait(held.at[m], hop_s.at[m])


def local(sizes, hidden_in, gains, weights, lengths):
    replicas, sections, groups = sizes
    slots, width = hidden_in.shape
    page = weights.shape[3]
    slabs = slots // ROWS
    near_z, near_x = replicas // NEAR_Y, groups // CORES
    share = replicas // CORES
    block = share * ROWS + ROWS
    bf16, f32 = jnp.bfloat16, jnp.float32
    dma = pltpu.SemaphoreType.DMA
    states = pl.pallas_call(
        functools.partial(kernel, (*sizes, slabs)),
        out_shape=jax.ShapeDtypeStruct((slots, width), bf16),
        in_specs=[pl.BlockSpec(memory_space=pltpu.VMEM)] * 3,
        out_specs=pl.BlockSpec(memory_space=pltpu.VMEM),
        scratch_shapes=[
            pltpu.VMEM((slabs, ROWS, width), bf16),
            pltpu.VMEM((slabs, NEAR_Y, near_z, ROWS, width), bf16),
            pltpu.VMEM((slabs, ROWS, LANES), f32),
            pltpu.VMEM((slabs, share * ROWS, page), f32),
            pltpu.VMEM((slabs, block, page), bf16),
            pltpu.VMEM((slabs, block, page), bf16),
            pltpu.VMEM((slabs, near_x, block, LANES), bf16),
            pltpu.VMEM((slabs, near_x - 1, block, LANES), bf16),
            pltpu.VMEM((slabs, share, ROWS, LANES), bf16),
            pltpu.VMEM((slabs, replicas, ROWS, LANES), bf16),
            pltpu.VMEM((slabs, ROWS, LANES), f32),
            dma((slabs,)), dma((slabs,)),
            dma((slabs,)), dma((slabs,)),
            dma((slabs, 2)), dma((slabs, 2)),
            dma((slabs, 2)), dma((slabs, 2)),
            dma((slabs,)), dma((slabs,)),
            dma((slabs,)), dma((slabs,)),
            dma((slabs,)), dma((slabs,)),
        ],
        compiler_params=pltpu.CompilerParams(
            collective_id=0, has_side_effects=True, vmem_limit_bytes=40 << 20
        ),
        name="layer_sections",
    )(hidden_in, gains, weights.reshape(width, page))
    positions = jnp.arange(slots, dtype=jnp.int32)
    return jnp.where((positions < lengths[0])[:, None], states, jnp.zeros_like(states))[None]


def solution(mesh):
    sizes = tuple(mesh.shape[axis] for axis in ("replica", "section", "tp"))
    return jax.shard_map(
        functools.partial(local, sizes),
        mesh=mesh,
        in_specs=(
            P("replica", "tp"),
            P("section", "tp"),
            P("section", "tp", "replica", None),
            P("replica"),
        ),
        out_specs=P("section", "replica", "tp"),
        check_vma=False,
    )
```

time: 1130 us -> 185 us (0.16)
  waiting for transfers between devices: 898 us -> 0 us
  Pallas kernels: 0 us -> 181 us
  blocking collectives: 109 us -> 0 us
  starting transfers between devices: 57 us -> 0 us
  matrix products: 19.6 us -> 0 us
  local copies, waits for them, and re-layouts: 18.1 us -> 2.18 us
  between operations: 14.3 us -> 0.69 us
    all_gather x7 -> x0, waiting for transfers between devices: 477 us -> none  [local(): lax.all_gather(scaled, 'replica', axis=0, tiled=True)]
    reduce_scatter x7 -> x0, waiting for transfers between devices: 347 us -> none  [local(): lax.psum_scatter(partial_value.reshape(all_rows, groups, col_width).astyp...]
    pallas_call x0 -> x1, Pallas kernels: none -> 181 us  [local(): pl.pallas_call(functools.partial(kernel, (*sizes, slabs)), out_shape=jax....]
    psum x7 -> x0, blocking collectives: 109 us -> none  [local(): squares_sum = lax.psum(jnp.sum(widened * widened, axis=1), 'tp')]
    ppermute x6 -> x0, waiting for transfers between devices: 73.6 us -> none  [from_behind(): return lax.ppermute(block, axis, route)]
    all_to_all x7 -> x0, starting transfers between devices: 48.7 us -> none  [local(): lax.all_to_all(summed.reshape(all_rows, col_width).astype(jnp.bfloat16),...]
    dot_general x7 -> x0, matrix products: 19.6 us -> none  [local(): jnp.dot(lax.all_gather(scaled, 'replica', axis=0, tiled=True), w_local, p...]
  transfers between devices with their start and end apart: 27 -> 0, of which waited for: 20 -> 0; matrix products, arithmetic and copies ran while one was open for 0% -> 0% of each run, Pallas kernels for 0% -> 0%
where the time goes in v1:
time: 185 us; the launch traced here: 184 us
  Pallas kernels  181 us (98%)
  local copies, waits for them, and re-layouts  2.18 us (1%)
    pallas_call x1, Pallas kernels, local(): pl.pallas_call(functools.partial(kernel, (*sizes, slabs)), out_shape=jax....  181 us

profile of v1, /device:TPU:481, one launch (start us, length us, event | category | flops | bytes accessed | tf_op | source)
XLA Modules:
  0.0 184.3 jit_solution(8043836186828518392)
XLA Ops:
  0.0 0.0 copy-start.2
  0.7 0.0 copy-done.2
  0.7 0.0 copy-start
  0.7 1.2 copy-done
  1.9 0.0 copy-start.1
  1.9 0.9 copy-done.1
  2.9 180.6 %layer_sections.1 = bf16[128,1024]{1,0:T(8,128)(2,1)S(1)} custom-call(bf16[128,1024]{1,0:T(8,128)(2,1)S(1)} %copy-done.1, f32[1,1024]{1,0:T(1,128)S(1)} %copy-done.2, bf16[1024,512]{1,0:T(8,128)(2,1)S(1)} %bitcast.5), custom_call_target="tpu_custom_call" | custom-call | tf_op jit(solution)/shard_map/layer_sections/pallas_call | solution.py:230
  183.5 0.8 select_bitcast_fusion
  (1 shorter events, 0.0 us)
Async XLA Ops:
  0.0 0.7 copy-start.2
  0.7 1.2 copy-start
  1.9 0.9 copy-start.1

commit v2 on v0

v2 whole, which is shorter than its diff:
```python
import functools

import jax
import jax.numpy as jnp
from jax import lax
from jax.experimental import pallas as pl
from jax.experimental.pallas import tpu as pltpu
from jax.sharding import PartitionSpec as P

EPSILON = 1e-06
MESH = pl.DeviceIdType.MESH
NEAR_Y = 4
CORES = 2
ROWS = 8
HIGH = 16
LANES = 128
HALF = LANES // 2
BATCH = 2 * HIGH // ROWS

STAGES = dict(along_z=0.0, along_y=4, product=9, pair=10.5, update=14)
PAGES, PLACE = 14.1, 60
INTERVAL = 3


def order_of(slabs):
    events = [(m * INTERVAL + offset, m, name) for m in range(slabs) for name, offset in STAGES.items()]
    for batch in range(slabs // BATCH):
        last = (batch + 1) * BATCH - 1
        events += [(last * INTERVAL + PAGES, batch, "pages"), (last * INTERVAL + PLACE, batch, "place")]
    return [(name, index) for _, index, name in sorted(events, key=lambda e: (e[0], e[1]))]


def kernel(
    sizes, hid_hbm, gain_hbm, w_hbm, out_ref,
    hid_ref, gain_ref, w_ref,
    gathered, scaled, prod, residual, squares, mine, core_out, core_in, x_out, x_in, new_out, page_out, page_in,
    in_sem, hop_s, hop_r, z_s, z_r, e_s, e_r, y_s, y_r, c_s, c_r, x_s, x_r, p_s, p_r,
):
    replicas, sections, groups, slabs = sizes
    near_y, near_z, near_x = NEAR_Y, replicas // NEAR_Y, groups // CORES
    row_groups = replicas * ROWS // HIGH
    tiles = row_groups // 2
    width = hid_ref.shape[1]
    column_tiles = width // LANES
    bf16, f32 = jnp.bfloat16, jnp.float32

    replica, section, tp = lax.axis_index("replica"), lax.axis_index("section"), lax.axis_index("tp")
    z, y = replica // near_y, replica % near_y
    x, core = tp // CORES, tp % CORES

    def place_of(z_to=z, y_to=y, x_to=x, core_to=core, section_to=section):
        return (z_to * near_y + y_to, section_to, x_to * CORES + core_to)

    def send(src, dst, send_sem, recv_sem, device):
        pltpu.make_async_remote_copy(
            src_ref=src, dst_ref=dst, send_sem=send_sem, recv_sem=recv_sem, device_id=device, device_id_type=MESH
        ).start()

    def wait(ref, sem):
        pltpu.make_async_copy(ref, ref, sem).wait()

    lane = lax.broadcasted_iota(jnp.int32, (HIGH, LANES), 1)
    low = lane < HALF
    high_part = lane % 8 < 4

    def turn(value):
        return pltpu.roll(value, HALF, 1)

    def lows(left, right):
        return jnp.where(low, left, turn(right))

    def highs(left, right):
        return jnp.where(low, turn(left), right)

    def two_parts(value):
        high = value.astype(bf16).astype(f32)
        return jnp.where(high_part, high, value - high)

    def one_value(parts):
        return parts + jnp.where(high_part, pltpu.roll(parts, LANES - 4, 1), pltpu.roll(parts, 4, 1))

    def stack(above, below):
        return jnp.concatenate([above, below], axis=0)

    def slot_of(z_from):
        return (z_from - z + near_z) % near_z

    def load_hidden():
        return pltpu.make_async_copy(hid_hbm, hid_ref, in_sem.at[0])

    def load_gains():
        return pltpu.make_async_copy(gain_hbm, gain_ref, in_sem.at[1])

    def load_weights():
        return pltpu.make_async_copy(w_hbm, w_ref, in_sem.at[2])

    @pl.when(section == 0)
    def _():
        load_hidden().start()

    load_gains().start()
    load_weights().start()

    barrier = pltpu.get_barrier_semaphore()

    def greet(device):
        pl.semaphore_signal(barrier, inc=1, device_id=device, device_id_type=MESH)

    @pl.when(section > 0)
    def _():
        greet(place_of(section_to=section - 1))

    for dz in range(near_z):
        for dy in range(near_y):
            if dz or dy:
                greet(place_of((z + dz) % near_z, (y + dy) % near_y))
    greet(place_of(core_to=1 - core))
    for dx in range(1, near_x):
        greet(place_of(x_to=(x + dx) % near_x))

    @pl.when(section == 0)
    def _():
        load_hidden().wait()

        def of_pair(pair, _):
            rows = pl.ds(pl.multiple_of(pair * HIGH, HIGH), HIGH)
            for t in range(tiles):
                left = hid_ref[rows, pl.ds(t * LANES, LANES)].astype(f32)
                right = hid_ref[rows, pl.ds((t + tiles) * LANES, LANES)].astype(f32)
                gathered[2 * pair, y, 0, t] = stack(left[:ROWS], right[:ROWS]).astype(bf16)
                gathered[2 * pair + 1, y, 0, t] = stack(left[ROWS:], right[ROWS:]).astype(bf16)
            return 0

        lax.fori_loop(0, slabs // 2, of_pair, 0)

    pl.semaphore_wait(barrier, replicas + near_x - 1 + jnp.where(section < sections - 1, 1, 0))

    def along_z(m):
        block = gathered.at[m, y, 0]

        @pl.when(section > 0)
        def _():
            wait(block, hop_r.at[m])

        for dz in range(1, near_z):
            send(block, gathered.at[m, y, near_z - dz], z_s.at[m], z_r.at[m], place_of(z_to=(z + dz) % near_z))
        for dy in range(1, near_y):
            send(block, block, e_s.at[m], e_r.at[m], place_of(y_to=(y + dy) % near_y))

    def along_y(m):
        block = gathered.at[m, y, pl.ds(1, near_z - 1)]
        wait(block, z_r.at[m])
        for dy in range(1, near_y):
            send(block, block, y_s.at[m], y_r.at[m], place_of(y_to=(y + dy) % near_y))

    def product(m):
        wait(gathered.at[m, pl.ds(0, near_y - 1), 0], e_r.at[m])
        wait(gathered.at[m, pl.ds(0, near_y - 1), pl.ds(1, near_z - 1)], y_r.at[m])

        def add_square(total, group, value):
            return total + jnp.where(lane // 8 == group, jnp.sum(value, axis=1, keepdims=True), 0.0)

        @pl.when(section == 0)
        def _():
            def chunks(group):
                y_from, z_from = 2 * group // near_z, 2 * group % near_z
                return y_from, slot_of(z_from), slot_of(z_from + 1)

            def of_group(group, total):
                y_from, first, second = chunks(group)
                acc = jnp.zeros((HIGH, LANES), f32)
                rows = pl.ds(pl.multiple_of(group * HIGH, HIGH), HIGH)
                for t in range(tiles):
                    one = gathered[m, y_from, first, t].astype(f32)
                    two = gathered[m, y_from, second, t].astype(f32)
                    for k, value in ((t, stack(one[:ROWS], two[:ROWS])), (t + tiles, stack(one[ROWS:], two[ROWS:]))):
                        columns = pl.ds(k * LANES, LANES)
                        acc += value * value
                        scaled[rows, columns] = (value * gain_ref[:, columns]).astype(bf16)
                return add_square(total, group, acc)

            squares[m] = two_parts(lax.fori_loop(0, row_groups, of_group, jnp.zeros((HIGH, LANES), f32)))
            odd = replica % 2 == 1
            column = replica // 2
            upper = column >= tiles

            def own_columns(group):
                y_from, first, second = chunks(group)
                one = gathered[m, y_from, first, column % tiles].astype(f32)
                two = gathered[m, y_from, second, column % tiles].astype(f32)
                return jnp.where(upper, stack(one[ROWS:], two[ROWS:]), stack(one[:ROWS], two[:ROWS]))

            for a in range(tiles):
                left, right = own_columns(a), own_columns(a + tiles)
                residual[m, a] = jnp.where(odd, highs(left, right), lows(left, right)).astype(bf16)

        @pl.when(section > 0)
        def _():
            def of_tile(a, total):
                acc = jnp.zeros((HIGH, LANES), f32)
                top = pl.ds(pl.multiple_of(a * HIGH, HIGH), HIGH)
                bottom = pl.ds(pl.multiple_of((a + tiles) * HIGH, HIGH), HIGH)
                for k in range(column_tiles):
                    columns = pl.ds(k * LANES, LANES)
                    gain = gain_ref[:, columns]
                    y_from, slot = 2 * k % near_y, slot_of(2 * k // near_y)
                    left = gathered[m, y_from, slot, a].astype(f32)
                    right = gathered[m, y_from + 1, slot, a].astype(f32)
                    acc += left * left + right * right
                    scaled[top, columns] = (lows(left, right) * gain).astype(bf16)
                    scaled[bottom, columns] = (highs(left, right) * gain).astype(bf16)
                total = add_square(total, a, jnp.where(low, acc, 0.0))
                return add_square(total, a + tiles, jnp.where(low, 0.0, acc))

            squares[m] = two_parts(lax.fori_loop(0, tiles, of_tile, jnp.zeros((HIGH, LANES), f32)))
            residual[m] = gathered[m, y, 0]

        prod[...] = jnp.dot(scaled[...], w_ref[...], preferred_element_type=f32)
        first_core = core == 0

        def split(a, _):
            top = pl.ds(pl.multiple_of(a * HIGH, HIGH), HIGH)
            bottom = pl.ds(pl.multiple_of((a + tiles) * HIGH, HIGH), HIGH)
            for j in range(near_x):
                columns = pl.ds(j * LANES, LANES)
                left, right = prod[top, columns], prod[bottom, columns]
                of_0, of_1 = lows(left, right), highs(left, right)
                mine[m, j, a] = jnp.where(first_core, of_0, of_1)
                core_out[m, j * tiles + a] = jnp.where(first_core, of_1, of_0).astype(bf16)
            return 0

        lax.fori_loop(0, tiles, split, 0)
        core_out[m, near_x * tiles] = squares[m].astype(bf16)
        send(core_out.at[m], core_in.at[m], c_s.at[m], c_r.at[m], place_of(core_to=1 - core))

    def pair(m):
        wait(core_in.at[m], c_r.at[m])
        parts = squares[m] + core_in[m, near_x * tiles].astype(f32)
        parts = two_parts(one_value(parts)).astype(bf16)
        for j in range(near_x):
            theirs = core_in[m, pl.ds(j * tiles, tiles)].astype(f32)
            x_out[m, j, pl.ds(0, tiles)] = (mine[m, j] + theirs).astype(bf16)
            x_out[m, j, tiles] = parts
        for dx in range(1, near_x):
            to = (x + dx) % near_x
            send(x_out.at[m, to], x_in.at[m, dx - 1], x_s.at[m], x_r.at[m], place_of(x_to=to))

    def update(m):
        wait(x_in.at[m], x_r.at[m])

        def total(a):
            value = x_out[m, x, a].astype(f32)
            for dx in range(1, near_x):
                value += x_in[m, dx - 1, a].astype(f32)
            return value

        inverse = lax.rsqrt(one_value(total(tiles)) / (width * groups) + EPSILON)
        for a in range(tiles):
            b = a + tiles
            factor = jnp.where(low, inverse[:, 8 * a : 8 * a + 1], inverse[:, 8 * b : 8 * b + 1])
            new_out[m, a] = (residual[m, a].astype(f32) + factor * total(a)).astype(bf16)

        @pl.when(section < sections - 1)
        def _():
            send(new_out.at[m], gathered.at[m, y, 0], hop_s.at[m], hop_r.at[m], place_of(section_to=section + 1))

    def pages(batch):
        for q in range(replicas):
            group, part = q * ROWS // HIGH, q * ROWS % HIGH
            piece = [
                new_out[batch * BATCH + i, group % tiles].astype(f32)[part : part + ROWS] for i in range(BATCH)
            ]
            left, right = stack(piece[0], piece[1]), stack(piece[2], piece[3])
            page_out[batch, q] = (lows if group < tiles else highs)(left, right).astype(bf16)
            y_to, z_to = q // near_z, q % near_z
            src, dst = page_out.at[batch, q], page_in.at[batch, replica]
            here = (z_to == z) & (y_to == y)

            @pl.when(here)
            def _(src=src, dst=dst):
                pltpu.make_async_copy(src, dst, p_r.at[batch]).start()

            @pl.when(jnp.logical_not(here))
            def _(src=src, dst=dst, z_to=z_to, y_to=y_to):
                send(src, dst, p_s.at[batch], p_r.at[batch], place_of(z_to, y_to))

    def place(batch):
        wait(page_in.at[batch], p_r.at[batch])
        row = batch * BATCH * ROWS
        for k in range(column_tiles):
            columns = pl.ds(k * LANES, LANES)
            left, right = page_in[batch, 2 * k].astype(f32), page_in[batch, 2 * k + 1].astype(f32)
            out_ref[pl.ds(row, HIGH), columns] = lows(left, right).astype(bf16)
            out_ref[pl.ds(row + HIGH, HIGH), columns] = highs(left, right).astype(bf16)

    stages = dict(
        along_z=along_z, along_y=along_y, product=product, pair=pair, update=update, pages=pages, place=place
    )
    loaded = False
    for name, index in order_of(slabs):
        if name == "product" and not loaded:
            load_gains().wait()
            load_weights().wait()
            loaded = True
        stages[name](index)

    for m in range(slabs):
        wait(gathered.at[m, 0, pl.ds(1, near_z - 1)], z_s.at[m])
        wait(gathered.at[m, pl.ds(0, near_y - 1), 0], e_s.at[m])
        wait(gathered.at[m, pl.ds(0, near_y - 1), pl.ds(1, near_z - 1)], y_s.at[m])
        wait(core_out.at[m], c_s.at[m])
        wait(x_in.at[m], x_s.at[m])

        @pl.when(section < sections - 1)
        def _(m=m):
            wait(new_out.at[m], hop_s.at[m])

    for batch in range(slabs // BATCH):
        wait(page_in.at[batch, pl.ds(0, replicas - 1)], p_s.at[batch])


def local(sizes, hidden_in, gains, weights, lengths):
    replicas, sections, groups = sizes
    slots, width = hidden_in.shape
    page = weights.shape[3]
    slabs = slots // ROWS
    batches = slabs // BATCH
    near_z, near_x = replicas // NEAR_Y, groups // CORES
    rows = replicas * ROWS
    tiles = rows // HIGH // 2
    bf16, f32 = jnp.bfloat16, jnp.float32
    tile = (HIGH, LANES)
    dma = pltpu.SemaphoreType.DMA
    states = pl.pallas_call(
        functools.partial(kernel, (*sizes, slabs)),
        out_shape=jax.ShapeDtypeStruct((slots, width), bf16),
        in_specs=[pl.BlockSpec(memory_space=pl.ANY)] * 3,
        out_specs=pl.BlockSpec(memory_space=pltpu.VMEM),
        scratch_shapes=[
            pltpu.VMEM((slots, width), bf16),
            pltpu.VMEM((1, width), f32),
            pltpu.VMEM((width, page), bf16),
            pltpu.VMEM((slabs, NEAR_Y, near_z, tiles, *tile), bf16),
            pltpu.VMEM((rows, width), bf16),
            pltpu.VMEM((rows, page), f32),
            pltpu.VMEM((slabs, tiles, *tile), bf16),
            pltpu.VMEM((slabs, *tile), f32),
            pltpu.VMEM((slabs, near_x, tiles, *tile), f32),
            pltpu.VMEM((slabs, near_x * tiles + 1, *tile), bf16),
            pltpu.VMEM((slabs, near_x * tiles + 1, *tile), bf16),
            pltpu.VMEM((slabs, near_x, tiles + 1, *tile), bf16),
            pltpu.VMEM((slabs, near_x - 1, tiles + 1, *tile), bf16),
            pltpu.VMEM((slabs, tiles, *tile), bf16),
            pltpu.VMEM((batches, replicas, *tile), bf16),
            pltpu.VMEM((batches, replicas, *tile), bf16),
            dma((3,)),
            *[dma((slabs,))] * 12,
            *[dma((batches,))] * 2,
        ],
        compiler_params=pltpu.CompilerParams(
            collective_id=0, has_side_effects=True, vmem_limit_bytes=56 << 20
        ),
        name="layer_sections",
    )(hidden_in, gains, weights.reshape(width, page))
    positions = jnp.arange(slots, dtype=jnp.int32)
    return jnp.where((positions < lengths[0])[:, None], states, jnp.zeros_like(states))[None]


def solution(mesh):
    sizes = tuple(mesh.shape[axis] for axis in ("replica", "section", "tp"))
    return jax.shard_map(
        functools.partial(local, sizes),
        mesh=mesh,
        in_specs=(
            P("replica", "tp"),
            P("section", "tp"),
            P("section", "tp", "replica", None),
            P("replica"),
        ),
        out_specs=P("section", "replica", "tp"),
        check_vma=False,
    )
```

time: 1130 us -> 147 us (0.13)
  waiting for transfers between devices: 898 us -> 0 us
  Pallas kernels: 0 us -> 144 us
  blocking collectives: 109 us -> 0 us
  starting transfers between devices: 57 us -> 0 us
  matrix products: 19.6 us -> 0 us
  local copies, waits for them, and re-layouts: 18.1 us -> 0 us
  between operations: 14.3 us -> 0.67 us
    all_gather x7 -> x0, waiting for transfers between devices: 477 us -> none  [local(): lax.all_gather(scaled, 'replica', axis=0, tiled=True)]
    reduce_scatter x7 -> x0, waiting for transfers between devices: 347 us -> none  [local(): lax.psum_scatter(partial_value.reshape(all_rows, groups, col_width).astyp...]
    pallas_call x0 -> x1, Pallas kernels: none -> 144 us  [local(): pl.pallas_call(functools.partial(kernel, (*sizes, slabs)), out_shape=jax....]
    psum x7 -> x0, blocking collectives: 109 us -> none  [local(): squares_sum = lax.psum(jnp.sum(widened * widened, axis=1), 'tp')]
    ppermute x6 -> x0, waiting for transfers between devices: 73.6 us -> none  [from_behind(): return lax.ppermute(block, axis, route)]
    all_to_all x7 -> x0, starting transfers between devices: 48.7 us -> none  [local(): lax.all_to_all(summed.reshape(all_rows, col_width).astype(jnp.bfloat16),...]
    dot_general x7 -> x0, matrix products: 19.6 us -> none  [local(): jnp.dot(lax.all_gather(scaled, 'replica', axis=0, tiled=True), w_local, p...]
  transfers between devices with their start and end apart: 27 -> 0, of which waited for: 20 -> 0; matrix products, arithmetic and copies ran while one was open for 0% -> 0% of each run, Pallas kernels for 0% -> 0%
where the time goes in v2:
time: 147 us; the launch traced here: 146 us
  Pallas kernels  144 us (98%)
  other arithmetic  1.75 us (1%)
    pallas_call x1, Pallas kernels, local(): pl.pallas_call(functools.partial(kernel, (*sizes, slabs)), out_shape=jax....  144 us

profile of v2, /device:TPU:481, one launch (start us, length us, event | category | flops | bytes accessed | tf_op | source)
XLA Modules:
  0.0 146.3 jit_solution(478591515626558157)
XLA Ops:
  0.7 143.9 %layer_sections.1 = bf16[128,1024]{1,0:T(8,128)(2,1)} custom-call(bf16[128,1024]{1,0:T(8,128)(2,1)} %hid_hbm.1, f32[1,1024]{1,0:T(1,128)} %gain_hbm.1, bf16[1024,512]{1,0:T(8,128)(2,1)} %bitcast.5), custom_call_target="tpu_custom_call" | custom-call | tf_op jit(solution)/shard_map/layer_sections/pallas_call | solution.py:334
  144.5 1.7 %select_bitcast_fusion = bf16[1,128,1024]{2,1,0:T(8,128)(2,1)} fusion(bf16[128,1024]{1,0:T(8,128)(2,1)} %layer_sections.1, pred[128]{0:T(512)(128)(4,1)S(1)} %iota_compare_fusion), kind=kLoop, calls=%fused_computation | loop fusion | flops 131072 | bytes 524416 | tf_op jit(solution)/shard_map/broadcast_in_dim | solution.py:366
  (1 shorter events, 0.0 us)

commit v3 on v2

--- a/solution.py
+++ b/solution.py
@@ -32,15 +32,15 @@
 
 def kernel(
     sizes, hid_hbm, gain_hbm, w_hbm, out_ref,
-    hid_ref, gain_ref, w_ref,
-    gathered, scaled, prod, residual, squares, mine, core_out, core_in, x_out, x_in, new_out, page_out, page_in,
+    hid_ref, gain_ref, w_raw, w_ref, ones,
+    gathered, rows_in, residual, squares, mine, core_out, core_in, x_out, x_in, new_out, page_out, page_in,
     in_sem, hop_s, hop_r, z_s, z_r, e_s, e_r, y_s, y_r, c_s, c_r, x_s, x_r, p_s, p_r,
 ):
     replicas, sections, groups, slabs = sizes
     near_y, near_z, near_x = NEAR_Y, replicas // NEAR_Y, groups // CORES
     row_groups = replicas * ROWS // HIGH
     tiles = row_groups // 2
-    width = hid_ref.shape[1]
+    width, page = w_raw.shape
     column_tiles = width // LANES
     bf16, f32 = jnp.bfloat16, jnp.float32
 
@@ -92,7 +92,7 @@
         return pltpu.make_async_copy(gain_hbm, gain_ref, in_sem.at[1])
 
     def load_weights():
-        return pltpu.make_async_copy(w_hbm, w_ref, in_sem.at[2])
+        return pltpu.make_async_copy(w_hbm, w_raw, in_sem.at[2])
 
     @pl.when(section == 0)
     def _():
@@ -153,33 +153,46 @@
         for dy in range(1, near_y):
             send(block, block, y_s.at[m], y_r.at[m], place_of(y_to=(y + dy) % near_y))
 
+    def prepare():
+        load_gains().wait()
+        load_weights().wait()
+        ones[...] = jnp.ones_like(ones)
+        wide_low = lax.broadcasted_iota(jnp.int32, (LANES, LANES), 1) < HALF
+
+        def of_rows(k, _):
+            rows = pl.ds(pl.multiple_of(k * LANES, LANES), LANES)
+            gain = jnp.transpose(jnp.broadcast_to(gain_ref[:, rows], (LANES, LANES)))
+            for j in range(near_x // 2):
+                left = w_raw[rows, pl.ds(2 * j * LANES, LANES)].astype(f32) * gain
+                right = w_raw[rows, pl.ds((2 * j + 1) * LANES, LANES)].astype(f32) * gain
+                of_0 = jnp.where(wide_low, left, turn(right))
+                of_1 = jnp.where(wide_low, turn(left), right)
+                w_ref[rows, pl.ds(j * LANES, LANES)] = of_0.astype(bf16)
+                w_ref[rows, pl.ds((near_x // 2 + j) * LANES, LANES)] = of_1.astype(bf16)
+            return 0
+
+        lax.fori_loop(0, column_tiles, of_rows, 0)
+
     def product(m):
         wait(gathered.at[m, pl.ds(0, near_y - 1), 0], e_r.at[m])
         wait(gathered.at[m, pl.ds(0, near_y - 1), pl.ds(1, near_z - 1)], y_r.at[m])
-
-        def add_square(total, group, value):
-            return total + jnp.where(lane // 8 == group, jnp.sum(value, axis=1, keepdims=True), 0.0)
+        slots = [slot_of(z_from) for z_from in range(near_z)]
 
         @pl.when(section == 0)
         def _():
             def chunks(group):
                 y_from, z_from = 2 * group // near_z, 2 * group % near_z
-                return y_from, slot_of(z_from), slot_of(z_from + 1)
-
-            def of_group(group, total):
+                return y_from, slots[z_from], slots[z_from + 1]
+
+            for group in range(row_groups):
                 y_from, first, second = chunks(group)
-                acc = jnp.zeros((HIGH, LANES), f32)
-                rows = pl.ds(pl.multiple_of(group * HIGH, HIGH), HIGH)
+                rows = pl.ds(group * HIGH, HIGH)
                 for t in range(tiles):
                     one = gathered[m, y_from, first, t].astype(f32)
                     two = gathered[m, y_from, second, t].astype(f32)
-                    for k, value in ((t, stack(one[:ROWS], two[:ROWS])), (t + tiles, stack(one[ROWS:], two[ROWS:]))):
-                        columns = pl.ds(k * LANES, LANES)
-                        acc += value * value
-                        scaled[rows, columns] = (value * gain_ref[:, columns]).astype(bf16)
-                return add_square(total, group, acc)
-
-            squares[m] = two_parts(lax.fori_loop(0, row_groups, of_group, jnp.zeros((HIGH, LANES), f32)))
+                    rows_in[rows, pl.ds(t * LANES, LANES)] = stack(one[:ROWS], two[:ROWS]).astype(bf16)
+                    rows_in[rows, pl.ds((t + tiles) * LANES, LANES)] = stack(one[ROWS:], two[ROWS:]).astype(bf16)
+
             odd = replica % 2 == 1
             column = replica // 2
             upper = column >= tiles
@@ -196,50 +209,49 @@
 
         @pl.when(section > 0)
         def _():
-            def of_tile(a, total):
-                acc = jnp.zeros((HIGH, LANES), f32)
-                top = pl.ds(pl.multiple_of(a * HIGH, HIGH), HIGH)
-                bottom = pl.ds(pl.multiple_of((a + tiles) * HIGH, HIGH), HIGH)
+            for a in range(tiles):
+                top, bottom = pl.ds(a * HIGH, HIGH), pl.ds((a + tiles) * HIGH, HIGH)
                 for k in range(column_tiles):
                     columns = pl.ds(k * LANES, LANES)
-                    gain = gain_ref[:, columns]
-                    y_from, slot = 2 * k % near_y, slot_of(2 * k // near_y)
-                    left = gathered[m, y_from, slot, a].astype(f32)
-                    right = gathered[m, y_from + 1, slot, a].astype(f32)
-                    acc += left * left + right * right
-                    scaled[top, columns] = (lows(left, right) * gain).astype(bf16)
-                    scaled[bottom, columns] = (highs(left, right) * gain).astype(bf16)
-                total = add_square(total, a, jnp.where(low, acc, 0.0))
-                return add_square(total, a + tiles, jnp.where(low, 0.0, acc))
-
-            squares[m] = two_parts(lax.fori_loop(0, tiles, of_tile, jnp.zeros((HIGH, LANES), f32)))
+                    y_from, slot = 2 * k % near_y, slots[2 * k // near_y]
+                    left = gathered[m, y_from, slot, a]
+                    right = gathered[m, y_from + 1, slot, a]
+                    rows_in[top, columns] = jnp.concatenate([left[:, :HALF], right[:, :HALF]], axis=1)
+                    rows_in[bottom, columns] = jnp.concatenate([left[:, HALF:], right[:, HALF:]], axis=1)
+
             residual[m] = gathered[m, y, 0]
 
-        prod[...] = jnp.dot(scaled[...], w_ref[...], preferred_element_type=f32)
-        first_core = core == 0
-
-        def split(a, _):
-            top = pl.ds(pl.multiple_of(a * HIGH, HIGH), HIGH)
-            bottom = pl.ds(pl.multiple_of((a + tiles) * HIGH, HIGH), HIGH)
-            for j in range(near_x):
-                columns = pl.ds(j * LANES, LANES)
-                left, right = prod[top, columns], prod[bottom, columns]
-                of_0, of_1 = lows(left, right), highs(left, right)
-                mine[m, j, a] = jnp.where(first_core, of_0, of_1)
-                core_out[m, j * tiles + a] = jnp.where(first_core, of_1, of_0).astype(bf16)
-            return 0
-
-        lax.fori_loop(0, tiles, split, 0)
-        core_out[m, near_x * tiles] = squares[m].astype(bf16)
+        value = rows_in[...]
+        all_squares = jnp.dot(value * value, ones[...], preferred_element_type=f32)
+        parts = jnp.zeros((HIGH, LANES), f32)
+        for group in range(row_groups):
+            parts = jnp.where(lane // 8 == group, all_squares[group * HIGH : (group + 1) * HIGH], parts)
+        squares[m] = two_parts(parts)
+        core_out[m, row_groups * near_x // 2] = squares[m].astype(bf16)
+        theirs = pl.ds(pl.multiple_of((1 - core) * (page // 2), page // 2), page // 2)
+        result = jnp.dot(value, w_ref[:, theirs], preferred_element_type=f32).astype(bf16)
+        for k in range(near_x // 2):
+            core_out[m, pl.ds(k * row_groups, row_groups)] = result[:, k * LANES : (k + 1) * LANES].reshape(
+                row_groups, HIGH, LANES
+            )
         send(core_out.at[m], core_in.at[m], c_s.at[m], c_r.at[m], place_of(core_to=1 - core))
+        own = pl.ds(pl.multiple_of(core * (page // 2), page // 2), page // 2)
+        mine[m] = jnp.dot(value, w_ref[:, own], preferred_element_type=f32)
 
     def pair(m):
         wait(core_in.at[m], c_r.at[m])
-        parts = squares[m] + core_in[m, near_x * tiles].astype(f32)
+        parts = squares[m] + core_in[m, row_groups * near_x // 2].astype(f32)
         parts = two_parts(one_value(parts)).astype(bf16)
+        for k in range(near_x // 2):
+            def total(group):
+                rows, columns = pl.ds(group * HIGH, HIGH), pl.ds(k * LANES, LANES)
+                return mine[m, rows, columns] + core_in[m, k * row_groups + group].astype(f32)
+
+            for a in range(tiles):
+                left, right = total(a), total(a + tiles)
+                x_out[m, 2 * k, a] = lows(left, right).astype(bf16)
+                x_out[m, 2 * k + 1, a] = highs(left, right).astype(bf16)
         for j in range(near_x):
-            theirs = core_in[m, pl.ds(j * tiles, tiles)].astype(f32)
-            x_out[m, j, pl.ds(0, tiles)] = (mine[m, j] + theirs).astype(bf16)
             x_out[m, j, tiles] = parts
         for dx in range(1, near_x):
             to = (x + dx) % near_x
@@ -299,8 +311,7 @@
     loaded = False
     for name, index in order_of(slabs):
         if name == "product" and not loaded:
-            load_gains().wait()
-            load_weights().wait()
+            prepare()
             loaded = True
         stages[name](index)
 
@@ -340,12 +351,13 @@
             pltpu.VMEM((slots, width), bf16),
             pltpu.VMEM((1, width), f32),
             pltpu.VMEM((width, page), bf16),
+            pltpu.VMEM((width, page), bf16),
+            pltpu.VMEM((width, LANES), bf16),
             pltpu.VMEM((slabs, NEAR_Y, near_z, tiles, *tile), bf16),
             pltpu.VMEM((rows, width), bf16),
-            pltpu.VMEM((rows, page), f32),
             pltpu.VMEM((slabs, tiles, *tile), bf16),
             pltpu.VMEM((slabs, *tile), f32),
-            pltpu.VMEM((slabs, near_x, tiles, *tile), f32),
+            pltpu.VMEM((slabs, rows, page // 2), f32),
             pltpu.VMEM((slabs, near_x * tiles + 1, *tile), bf16),
             pltpu.VMEM((slabs, near_x * tiles + 1, *tile), bf16),
             pltpu.VMEM((slabs, near_x, tiles + 1, *tile), bf16),

time: 147 us -> 141 us (0.959)
  Pallas kernels: 144 us -> 137 us
    pallas_call x1, Pallas kernels: 144 us -> 137 us  [local(): pl.pallas_call(functools.partial(kernel, (*sizes, slabs)), out_shape=jax....]
where the time goes in v3:
time: 141 us; the launch traced here: 140 us
  Pallas kernels  137 us (97%)
  other arithmetic  1.75 us (1%)
    pallas_call x1, Pallas kernels, local(): pl.pallas_call(functools.partial(kernel, (*sizes, slabs)), out_shape=jax....  137 us

profile of v3, /device:TPU:481, one launch (start us, length us, event | category | flops | bytes accessed | tf_op | source)
XLA Modules:
  0.0 139.7 jit_solution(1653504953628279051)
XLA Ops:
  0.7 137.3 %layer_sections.1 = bf16[128,1024]{1,0:T(8,128)(2,1)} custom-call(bf16[128,1024]{1,0:T(8,128)(2,1)} %hid_hbm.1, f32[1,1024]{1,0:T(1,128)} %gain_hbm.1, bf16[1024,512]{1,0:T(8,128)(2,1)} %bitcast.5), custom_call_target="tpu_custom_call" | custom-call | tf_op jit(solution)/shard_map/layer_sections/pallas_call | solution.py:345
  138.0 1.7 %select_bitcast_fusion = bf16[1,128,1024]{2,1,0:T(8,128)(2,1)} fusion(bf16[128,1024]{1,0:T(8,128)(2,1)} %layer_sections.1, pred[128]{0:T(512)(128)(4,1)S(1)} %iota_compare_fusion), kind=kLoop, calls=%fused_computation | loop fusion | flops 131072 | bytes 524416 | tf_op jit(solution)/shard_map/broadcast_in_dim | solution.py:378
  (1 shorter events, 0.0 us)

commit v4 on v3

--- a/solution.py
+++ b/solution.py
@@ -144,13 +144,13 @@
 
         for dz in range(1, near_z):
             send(block, gathered.at[m, y, near_z - dz], z_s.at[m], z_r.at[m], place_of(z_to=(z + dz) % near_z))
-        for dy in range(1, near_y):
+        for dy in (2, 1, near_y - 1):
             send(block, block, e_s.at[m], e_r.at[m], place_of(y_to=(y + dy) % near_y))
 
     def along_y(m):
         block = gathered.at[m, y, pl.ds(1, near_z - 1)]
         wait(block, z_r.at[m])
-        for dy in range(1, near_y):
+        for dy in (2, 1, near_y - 1):
             send(block, block, y_s.at[m], y_r.at[m], place_of(y_to=(y + dy) % near_y))
 
     def prepare():
@@ -308,14 +308,7 @@
     stages = dict(
         along_z=along_z, along_y=along_y, product=product, pair=pair, update=update, pages=pages, place=place
     )
-    loaded = False
-    for name, index in order_of(slabs):
-        if name == "product" and not loaded:
-            prepare()
-            loaded = True
-        stages[name](index)
-
-    for m in range(slabs):
+    def sent(m):
         wait(gathered.at[m, 0, pl.ds(1, near_z - 1)], z_s.at[m])
         wait(gathered.at[m, pl.ds(0, near_y - 1), 0], e_s.at[m])
         wait(gathered.at[m, pl.ds(0, near_y - 1), pl.ds(1, near_z - 1)], y_s.at[m])
@@ -323,8 +316,19 @@
         wait(x_in.at[m], x_s.at[m])
 
         @pl.when(section < sections - 1)
-        def _(m=m):
+        def _():
             wait(new_out.at[m], hop_s.at[m])
+
+    loaded = False
+    order = order_of(slabs)
+    for step, (name, index) in enumerate(order):
+        if name == "product" and not loaded:
+            prepare()
+            loaded = True
+        if step == len(order) - 1:
+            for m in range(slabs):
+                sent(m)
+        stages[name](index)
 
     for batch in range(slabs // BATCH):
         wait(page_in.at[batch, pl.ds(0, replicas - 1)], p_s.at[batch])

time: 141 us -> 140 us (level)
  no operation moved by 1% of the time
where the time goes in v4:
time: 140 us; the launch traced here: 139 us
  Pallas kernels  137 us (98%)
  other arithmetic  1.75 us (1%)
    pallas_call x1, Pallas kernels, local(): pl.pallas_call(functools.partial(kernel, (*sizes, slabs)), out_shape=jax....  137 us

profile of v4, /device:TPU:481, one launch (start us, length us, event | category | flops | bytes accessed | tf_op | source)
XLA Modules:
  0.0 139.1 jit_solution(12806193781983954046)
XLA Ops:
  0.7 136.6 %layer_sections.1 = bf16[128,1024]{1,0:T(8,128)(2,1)} custom-call(bf16[128,1024]{1,0:T(8,128)(2,1)} %hid_hbm.1, f32[1,1024]{1,0:T(1,128)} %gain_hbm.1, bf16[1024,512]{1,0:T(8,128)(2,1)} %bitcast.5), custom_call_target="tpu_custom_call" | custom-call | tf_op jit(solution)/shard_map/layer_sections/pallas_call | solution.py:349
  137.3 1.7 %select_bitcast_fusion = bf16[1,128,1024]{2,1,0:T(8,128)(2,1)} fusion(bf16[128,1024]{1,0:T(8,128)(2,1)} %layer_sections.1, pred[128]{0:T(512)(128)(4,1)S(1)} %iota_compare_fusion), kind=kLoop, calls=%fused_computation | loop fusion | flops 131072 | bytes 524416 | tf_op jit(solution)/shard_map/broadcast_in_dim | solution.py:382
  (1 shorter events, 0.0 us)
